TPU v7x, 32 devices: a whole 2x2x4 slice. The times are simulated.
32 devices in a mesh: pipe: 4 (over y, x), ctx: 4 (over z), tp: 2 (over core).
Axes of the slice: x: 2, y: 2, z: 4, core: 2. Of those that a mesh axis runs over, the one named last changes fastest.
Arguments:
- q_self: bfloat16 [4, 1024, 4096], P('pipe', 'ctx', 'tp'), may hold values from -5 to 5
- kv_self: bfloat16 [4, 1024, 2, 512], P('pipe', 'ctx', None, 'tp'), may hold values from -5 to 5
- q_cross: bfloat16 [4, 1024, 4096], P('pipe', 'ctx', 'tp'), may hold values from -5 to 5
- kv_cross: bfloat16 [4, 2, 1024, 2, 512], P(None, None, ('pipe', 'ctx'), None, 'tp'), may hold values from -5 to 5
- sample_lengths: int32 [4, 8], P('pipe'), may hold values from 1 to 640, 1024 in all within a row
- sample_image: int32 [4, 8], P('pipe'), may hold values from 0 to 1
Outputs:
- self_out: bfloat16 [4, 1024, 4096], P('pipe', 'ctx', 'tp')
- cross_out: bfloat16 [4, 1024, 4096], P('pipe', 'ctx', 'tp')
Inputs may be any that keep to these rules, and one draw needn't show every extreme that they name: `sample_lengths`: each micro-batch's lengths sum to 1024; the longest sample of each micro-batch has exactly 640 positions.
All inputs are finite; a program needn't handle non-finite values.
Results may differ from a plain program's by a relative error of at most 0.0047.
Values may be sent and summed in bfloat16 or wider, within the bound.
No kernel may reach another device: no remote copies, remote signals or barrier semaphores. Data moves between devices by JAX's collectives and lax.ppermute only.
A program may use at most 128 MiB of HBM per device.

v0:
```python
import functools
import math

import jax
import jax.numpy as jnp
from jax import lax
from jax.experimental import pallas as pl
from jax.experimental.pallas import tpu as pltpu
from jax.sharding import PartitionSpec as P

HD = 128
TILE = 32
TOGETHER = 4
LOW = -1e30
EXP_SCALE = math.log2(math.e) / math.sqrt(HD)
NT = (((1,), (1,)), ((), ()))
NN = (((1,), (0,)), ((), ()))


def sample_bounds(lengths_ref, count):
    starts, ends, total = [], [], jnp.int32(0)
    for j in range(count):
        starts.append(total)
        total = total + lengths_ref[0, j]
        ends.append(total)
    return starts, ends


def stacked_queries(q_ref, tile, g, group):
    first = g * group
    rows = pl.ds(tile * TILE, TILE)
    return jnp.concatenate(
        [q_ref[rows, (first + h) * HD : (first + h + 1) * HD] for h in range(group)], axis=0
    )


def write_heads(out_ref, mixed, total, tile, g, group):
    rows = (mixed * (1.0 / total)).T.astype(out_ref.dtype)
    for h in range(group):
        at = (g * group + h) * HD
        out_ref[pl.ds(tile * TILE, TILE), at : at + HD] = rows[h * TILE : (h + 1) * TILE]


def scores_of(keys, q):
    return lax.dot_general(keys, q, NT, preferred_element_type=jnp.float32)


def absorb(state, s, v):
    if state is None:
        new_top = jnp.max(s, axis=0, keepdims=True)
    else:
        top, total, mixed = state
        new_top = jnp.maximum(top, jnp.max(s, axis=0, keepdims=True))
    w = jnp.exp2((s - new_top) * EXP_SCALE)
    added = jnp.sum(w, axis=0, keepdims=True)
    product = lax.dot_general(v, w.astype(jnp.bfloat16), NN, preferred_element_type=jnp.float32)
    if state is None:
        return new_top, added, product
    decay = jnp.exp2((top - new_top) * EXP_SCALE)
    return new_top, total * decay + added, mixed * decay + product


def staggered(units, score, finish):
    waiting = None
    for unit in units:
        s = score(*unit)
        if waiting is not None:
            finish(*waiting)
        waiting = (*unit, s)
    finish(*waiting)


def row_positions(first, height):
    return first + (lax.broadcasted_iota(jnp.int32, (1, height), 1) & (TILE - 1))


def lay(keys_at, flipped_at, ref, rows, kv_heads, g):
    keys_at[...] = ref[rows, g * HD : (g + 1) * HD]
    flipped_at[...] = ref[rows, (kv_heads + g) * HD : (kv_heads + g + 1) * HD].T


def self_kernel(
    lengths_ref, place_ref, q_ref, *refs, kv_heads, group, spans, parts, samples, begin, end
):
    refs = list(refs)
    take = lambda n: [refs.pop(0) for _ in range(n)]
    pieces = take(len({part[1] for part in parts}))
    stat_in, mixed_in = (None, None) if begin else take(2)
    out_ref = take(1)[0] if end else None
    stat_ref, mixed_ref, keys_ref, flipped_ref = take(4)
    rows_here = q_ref.shape[0]
    tiles = rows_here // TILE
    height = group * TILE
    base = place_ref[0] * rows_here
    _, ends = sample_bounds(lengths_ref, samples)
    ats = [sum(count for _, count in spans[:n]) for n in range(len(spans))]

    lows = []
    for tile in range(tiles):
        low = jnp.int32(0)
        for e in ends:
            low = jnp.where(e <= base + tile * TILE, e, low)
        lows.append(low)

    def limits(number):
        back, count = spans[number]
        past = base - (back - 1) * rows_here
        return past - count, past

    def reached(number):
        start, past = limits(number)
        many = jnp.int32(0)
        for low in lows:
            many = many + (low < past).astype(jnp.int32)
        return jnp.where(start >= 0, many, 0)

    counts = [reached(number) for number in range(len(spans))]
    for number, source, at, offset, count, only in parts:

        def fill(number=number, source=source, at=at, offset=offset, count=count):
            here = slice(ats[number] + offset, ats[number] + offset + count)
            for g in range(kv_heads):
                lay(
                    keys_ref.at[g, here], flipped_ref.at[g, :, here], pieces[source],
                    slice(at, at + count), kv_heads, g,
                )

        if spans[number][0] == 0:
            fill()
        else:
            asked = counts[number] > 0
            if only is not None:
                asked = asked & (place_ref[0] == only)
            pl.when(asked)(fill)

    def starts_of(first):
        row_t = row_positions(first, height)
        row_start = jnp.zeros((1, height), jnp.int32)
        for e in ends:
            row_start = jnp.where(e <= row_t, e, row_start)
        return row_start, row_t

    def keep(tile, g, state):
        stat_ref[tile, g, 0:1, :] = state[0]
        stat_ref[tile, g, 1:2, :] = state[1]
        mixed_ref[tile, g] = state[2]

    def own_count(tile):
        return min(rows_here, -(-(tile + 1) * TILE // HD) * HD)

    def own_scores(tile, g):
        q = stacked_queries(q_ref, tile, g, group)
        return scores_of(keys_ref[g, : own_count(tile)], q)

    def own_finish(tile, g, s):
        row_start, row_t = starts_of(base + tile * TILE)
        key_t = base + lax.broadcasted_iota(jnp.int32, (own_count(tile), 1), 0)
        s = jnp.where((key_t >= row_start) & (key_t <= row_t), s, LOW)
        keep(tile, g, absorb(None, s, flipped_ref[g, :, : own_count(tile)]))

    if begin:
        staggered(
            [(tile, g) for tile in range(tiles) for g in range(kv_heads)], own_scores, own_finish
        )
    else:
        stat_ref[...] = stat_in[...]
        mixed_ref[...] = mixed_in[...]

    together = math.gcd(tiles, TOGETHER)
    for number in range(1 if begin else 0, len(spans)):
        start, _ = limits(number)
        at, count = ats[number], spans[number][1]

        @pl.loop(0, (counts[number] + together - 1) // together)
        def _(turn, start=start, at=at, count=count):
            def scores(n, g):
                q = stacked_queries(q_ref, turn * together + n, g, group)
                return scores_of(keys_ref[g, at : at + count], q)

            def finish(n, g, s):
                tile = turn * together + n
                row_start, _ = starts_of(base + tile * TILE)
                key_t = start + lax.broadcasted_iota(jnp.int32, (count, 1), 0)
                s = jnp.where(key_t >= row_start, s, LOW)
                old = stat_ref[tile, g, 0:1, :], stat_ref[tile, g, 1:2, :], mixed_ref[tile, g]
                keep(tile, g, absorb(old, s, flipped_ref[g, :, at : at + count]))

            staggered(
                [(n, g) for n in range(together) for g in range(kv_heads)], scores, finish
            )

    for tile in range(tiles if end else 0):
        for g in range(kv_heads):
            write_heads(out_ref, mixed_ref[tile, g], stat_ref[tile, g, 1:2, :], tile, g, group)


def cross_kernel(
    lengths_ref, images_ref, place_ref, q_ref, *refs, kv_heads, group, sources, samples, begin, end
):
    refs = list(refs)
    take = lambda n: [refs.pop(0) for _ in range(n)]
    pieces = [take(len(source)) for source in sources]
    stat_in, mixed_in = (None, None) if begin else take(2)
    out_ref = take(1)[0] if end else None
    stat_ref, mixed_ref, keys_ref, flipped_ref = take(4)
    rows_ref, copied = take(2) if end else (None, None)
    rows_here = q_ref.shape[0]
    tiles = rows_here // TILE
    height = group * TILE
    base = place_ref[0] * rows_here
    starts, _ = sample_bounds(lengths_ref, samples)
    image_count = keys_ref.shape[0]

    def fill(ref, at, parts, each, only):
        for n in range(kv_heads):
            if only not in (None, n):
                continue
            k_at = n * HD if only is None else 0
            v_at = k_at + ref.shape[1] // 2
            for image in range(image_count):
                values = []
                for part in range(parts):
                    first = (part * image_count + image) * each
                    here = slice(at + part * each, at + (part + 1) * each)
                    keys_ref[image, n, here] = ref[first : first + each, k_at : k_at + HD]
                    values.append(ref[first : first + each, v_at : v_at + HD])
                whole = jnp.concatenate(values, axis=0)
                flipped_ref[image, n, :, at : at + parts * each] = whole.T

    at = 0
    for source, given in zip(sources, pieces):
        for number, ((parts, each, only), ref) in enumerate(zip(source, given)):
            put = functools.partial(fill, ref, at, parts, each, only)
            if len(source) == 1:
                put()
            else:
                pl.when(place_ref[1] == 1 - number)(put)
        if source[0][2] in (None, kv_heads - 1):
            at += source[0][0] * source[0][1]

    def images_of(tile):
        first = base + tile * TILE
        row_t = row_positions(first, height)
        row_image = jnp.zeros((1, height), jnp.int32)
        leading = jnp.int32(0)
        for j in range(samples):
            row_image = jnp.where(row_t >= starts[j], images_ref[0, j], row_image)
            leading = jnp.where(first >= starts[j], images_ref[0, j], leading)
        return row_image, leading

    def keep(tile, g, state):
        stat_ref[tile, g, 0:1, :] = state[0]
        stat_ref[tile, g, 1:2, :] = state[1]
        mixed_ref[tile, g] = state[2]

    def chosen(mine, new, old):
        if old is None:
            old = LOW, 0.0, 0.0
        return [jnp.where(mine, n, o) for n, o in zip(new, old)]

    marks = [images_of(tile) for tile in range(tiles)]
    order = range(kv_heads)

    def scores(tile, n):
        return scores_of(
            keys_ref[marks[tile][1], n], stacked_queries(q_ref, tile, n, group)
        )

    def finish(tile, n, s):
        row_image, leading = marks[tile]
        old = None
        if not begin:
            old = stat_in[tile, n, 0:1, :], stat_in[tile, n, 1:2, :], mixed_in[tile, n]
        new = absorb(old, s, flipped_ref[leading, n])
        keep(tile, n, chosen(row_image == leading, new, old))

    staggered([(tile, n) for tile in range(tiles) for n in order], scores, finish)

    @pl.loop(0, tiles)
    def _(tile):
        first = base + tile * TILE
        leading, others = jnp.int32(0), [jnp.bool_(False)] * image_count
        for j in range(samples):
            leading = jnp.where(first >= starts[j], images_ref[0, j], leading)
        for j in range(samples):
            inside = (starts[j] > first) & (starts[j] < first + TILE)
            for image in range(image_count):
                others[image] = others[image] | (inside & (images_ref[0, j] == image))
        for image in range(image_count):

            @pl.when(others[image] & (leading != image))
            def _(image=image):
                row_image, _ = images_of(tile)
                olds = [
                    (stat_ref[tile, n, 0:1, :], stat_ref[tile, n, 1:2, :], mixed_ref[tile, n])
                    for n in order
                ]
                ss = [
                    scores_of(keys_ref[image, n], stacked_queries(q_ref, tile, n, group))
                    for n in order
                ]
                for n in order:
                    new = absorb(olds[n], ss[n], flipped_ref[image, n])
                    keep(tile, n, chosen(row_image == image, new, olds[n]))

    if not end:
        return
    pace = 2
    copies = []
    for tile in range(tiles):
        for n in order:
            write_heads(rows_ref, mixed_ref[tile, n], stat_ref[tile, n, 1:2, :], tile, n, group)
        if (tile + 1) % pace == 0 or tile + 1 == tiles:
            done = slice(len(copies) * pace * TILE, (tile + 1) * TILE)
            copy = pltpu.make_async_copy(
                rows_ref.at[done], out_ref.at[done], copied.at[len(copies)]
            )
            copy.start()
            copies.append(copy)
    for copy in copies:
        copy.wait()


def smem():
    return pl.BlockSpec(memory_space=pltpu.SMEM)


def vmem():
    return pl.BlockSpec(memory_space=pltpu.VMEM)


def cost(rows, width, keys):
    return pl.CostEstimate(
        flops=8 * rows * width * keys, bytes_accessed=4 * rows * width,
        transcendentals=rows * (width // HD) * keys,
    )


def state_shapes(rows, kv_heads, group):
    tiles, height = rows // TILE, group * TILE
    return (tiles, kv_heads, 8, height), (tiles, kv_heads, HD, height)


def state_call(
    kernel, operands, rows, width, keys, shapes, scratch, end, dtype, placed=False
):
    scalars = sum(x.dtype == jnp.int32 for x in operands)
    state_scratch = []
    if end:
        out_shape = jax.ShapeDtypeStruct((rows, width), dtype)
        state_scratch = [pltpu.VMEM(s, jnp.float32) for s in shapes]
    else:
        out_shape = [jax.ShapeDtypeStruct(s, jnp.float32) for s in shapes]
    anywhere = pl.BlockSpec(memory_space=pl.ANY)
    in_specs = [smem()] * scalars + [vmem()] * (len(operands) - scalars)
    return pl.pallas_call(
        kernel,
        out_shape=out_shape,
        in_specs=in_specs,
        out_specs=(anywhere if placed else vmem()) if end else [vmem(), vmem()],
        scratch_shapes=state_scratch + scratch,
        compiler_params=pltpu.CompilerParams(vmem_limit_bytes=28 << 20),
        cost_estimate=cost(rows, width, keys),
    )(*operands)


def self_attention(lengths, place, q, pieces, spans, parts, state, end, kv_heads, group):
    rows, width = q.shape
    keys = sum(count for _, count in spans)
    begin = state is None
    kernel = functools.partial(
        self_kernel, kv_heads=kv_heads, group=group, spans=spans, parts=parts,
        samples=lengths.shape[1], begin=begin, end=end,
    )
    scratch = [
        pltpu.VMEM((kv_heads, keys, HD), q.dtype), pltpu.VMEM((kv_heads, HD, keys), q.dtype)
    ]
    operands = (lengths, place, q, *pieces, *(() if begin else state))
    shapes = state_shapes(rows, kv_heads, group)
    return state_call(kernel, operands, rows, width, keys, shapes, scratch, end, q.dtype)


def cross_attention(lengths, images, place, q, sources, state, end, kv_heads, group, image_count):
    rows, width = q.shape
    begin = state is None
    kernel = functools.partial(
        cross_kernel, kv_heads=kv_heads, group=group,
        sources=tuple(tuple(piece[1:] for piece in source) for source in sources),
        samples=lengths.shape[1], begin=begin, end=end,
    )
    pieces = [piece[0] for source in sources for piece in source]
    keys = sum(s[0][1] * s[0][2] for s in sources if s[0][3] in (None, 0))
    scratch = [
        pltpu.VMEM((image_count, kv_heads, keys, HD), q.dtype),
        pltpu.VMEM((image_count, kv_heads, HD, keys), q.dtype),
    ]
    if end:
        scratch += [pltpu.VMEM((rows, width), q.dtype), pltpu.SemaphoreType.DMA((rows // TILE,))]
    operands = (lengths, images, place, q, *pieces, *(() if begin else state))
    shapes = state_shapes(rows, kv_heads, group)
    return state_call(kernel, operands, rows, width, keys, shapes, scratch, end, q.dtype, True)


def per_device(q_self, kv_self, q_cross, kv_cross, sample_lengths, sample_image, *, n_pipe, n_ctx):
    rows = q_self.shape[1]
    kv_heads = kv_self.shape[3] // HD
    group = q_self.shape[2] // HD // kv_heads
    image_count, each = kv_cross.shape[1:3]
    z = lax.axis_index("ctx")
    inner = ((z == 1) | (z == 2)).astype(jnp.int32)
    place = jnp.stack([z, inner]).astype(jnp.int32)

    shift = lambda piece, step: lax.ppermute(
        piece, "ctx", [(c, c + 1) for c in range(step - 1, n_ctx - 1)]
    )
    passed = shift(kv_self[0], 1)
    arrived = lax.all_to_all(kv_cross, "pipe", split_axis=0, concat_axis=0, tiled=True)
    arrived, passed = lax.optimization_barrier((arrived, passed))
    flat = lambda array: array.reshape(-1, array.shape[-2] * array.shape[-1])
    own = flat(kv_self)
    longest = rows * n_ctx * 5 // 8

    attend_self = functools.partial(
        self_attention, sample_lengths, place, q_self[0], kv_heads=kv_heads, group=group
    )
    attend_cross = functools.partial(
        cross_attention, sample_lengths, sample_image, place, q_cross[0],
        kv_heads=kv_heads, group=group, image_count=image_count,
    )
    if n_ctx == 4:
        half = rows // 2
        at = lambda array, head=None: (array, n_pipe, each, head)
        near = lax.ppermute(arrived, "ctx", [(1, 2), (2, 1)])
        pair = lax.ppermute(arrived, "ctx", [(0, 1), (1, 0), (2, 3), (3, 2)])
        state = attend_cross([[at(flat(arrived))]], None, False)
        passed, state = lax.optimization_barrier((passed, state))
        two_back = lax.ppermute(passed, "ctx", [(1, 2), (2, 3)])
        three_back = lax.ppermute(passed[half:], "ctx", [(1, 3)])
        early = ((0, rows), (1, rows))
        parts = ((0, 0, 0, 0, rows, None), (1, 1, 0, 0, rows, None))
        self_state = attend_self([own, flat(passed)], early, parts, None, False)
        near, state = lax.optimization_barrier((near, state))
        pair, two_back, three_back, self_state = lax.optimization_barrier(
            (pair, two_back, three_back, self_state)
        )

        near = flat(near)
        near_on = lax.ppermute(near, "ctx", [(1, 0), (2, 3)])
        far = [
            lax.ppermute(flat(pair[..., g * HD : (g + 1) * HD]), "ctx", [(1, 2), (2, 1)])
            for g in range(kv_heads)
        ]
        state = attend_cross([[at(flat(pair))]], state, False)
        far[0], state = lax.optimization_barrier((far[0], state))
        late = ((2, rows), (3, half))
        parts = ((0, 0, 0, 0, rows, None), (1, 1, 0, 0, half, 3))
        self_out = attend_self([flat(two_back), flat(three_back)], late, parts, self_state, True)
        far_on = [lax.ppermute(part, "ctx", [(1, 0), (2, 3)]) for part in far]
        state = attend_cross([[at(near), at(near_on)]], state, False)
        last = [[at(far[g], g), at(far_on[g], g)] for g in range(kv_heads)]
        cross_out = attend_cross(last, state, True)
    else:
        pieces, spans = [own, flat(passed)], [(0, rows), (1, rows)]
        left, step = longest - 1 - rows, 1
        while left > 0 and step < n_ctx - 1:
            step += 1
            count = min(rows, -(-left // HD) * HD)
            pieces.append(shift(pieces[-1][rows - count :], step))
            spans.append((step, count))
            left -= rows
        parts = tuple((n, n, 0, 0, count, None) for n, (_, count) in enumerate(spans))
        self_out = attend_self(pieces, tuple(spans), parts, None, True)
        gathered = lax.all_gather(flat(arrived), "ctx", axis=0, tiled=True)
        cross_out = attend_cross([[(gathered, n_ctx * n_pipe, each, None)]], None, True)
    return self_out[None], cross_out[None]


def solution(mesh):
    in_specs = (
        P("pipe", "ctx", "tp"),
        P("pipe", "ctx", None, "tp"),
        P("pipe", "ctx", "tp"),
        P(None, None, ("pipe", "ctx"), None, "tp"),
        P("pipe", None),
        P("pipe", None),
    )
    out_specs = (P("pipe", "ctx", "tp"), P("pipe", "ctx", "tp"))
    body = functools.partial(
        per_device, n_pipe=mesh.shape["pipe"], n_ctx=mesh.shape["ctx"]
    )
    return jax.shard_map(
        body, mesh=mesh, in_specs=in_specs, out_specs=out_specs, check_vma=False
    )
```

profile of v0, /device:TPU:0, one launch (start us, length us, event | category | flops | bytes accessed | tf_op | source)
XLA Modules:
  0.0 66.2 jit_solution(4111877046721261124)
XLA Ops:
  0.6 0.0 copy-start.1
  0.6 0.0 copy-start.2
  0.7 0.0 copy-start
  0.7 5.3 %all-to-all-start = ((bf16[4,2,64,2,256]{4,3,2,1,0:T(2,128)(2,1)}), bf16[4,2,64,2,256]{4,3,2,1,0:T(2,128)(2,1)S(1)}, u32[]{:S(2)}, u32[]{:S(2)}) async-start(bf16[4,2,64,2,256]{4,3,2,1,0:T(2,128)(2,1)} %param.9), calls=%async_computation | async-start | bytes 1048576 | tf_op jit(solution)/shard_map/all_to_all | solution.py:417
  6.0 3.5 %collective-permute-start = (bf16[256,2,256]{2,1,0:T(2,128)(2,1)}, bf16[256,2,256]{2,1,0:T(2,128)(2,1)S(1)}, u32[]{:S(2)}, u32[]{:S(2)}) collective-permute-start(bf16[256,2,256]{2,1,0:T(2,128)(2,1)} %bitcast.55), channel_id=1, source_target_pairs={{0,2},{2,4},{4,6},{1,3},{3,5},{5,7},{8,10},{10,12},{12,14},{9,11},... | collective-permute-start | bytes 786440 | tf_op jit(solution)/shard_map/ppermute | solution.py:413
  9.5 5.6 %collective-permute-done = bf16[256,2,256]{2,1,0:T(2,128)(2,1)S(1)} collective-permute-done((bf16[256,2,256]{2,1,0:T(2,128)(2,1)}, bf16[256,2,256]{2,1,0:T(2,128)(2,1)S(1)}, u32[]{:S(2)}, u32[]{:S(2)}) %collective-permute-start) | collective-permute-done | bytes 262176 | tf_op jit(solution)/shard_map/ppermute | solution.py:413
  15.1 0.0 all-to-all-done
  15.1 1.5 %collective-permute-start.5 = (bf16[4,2,64,2,256]{4,3,2,1,0:T(2,128)(2,1)S(1)}, bf16[4,2,64,2,256]{4,3,2,1,0:T(2,128)(2,1)}, u32[]{:S(2)}, u32[]{:S(2)}) collective-permute-start(bf16[4,2,64,2,256]{4,3,2,1,0:T(2,128)(2,1)S(1)} %all-to-all-done), channel_id=1, source_target_pairs={{2,4},{4,2},{3,5},{5,3},{10,12},{12,10},{11,13},{13,11},{18,20},{2... | collective-permute-start | bytes 1572872 | tf_op jit(solution)/shard_map/ppermute | solution.py:433
  16.5 4.5 %collective-permute-start.1 = (bf16[4,2,64,2,256]{4,3,2,1,0:T(2,128)(2,1)S(1)}, bf16[4,2,64,2,256]{4,3,2,1,0:T(2,128)(2,1)S(1)}, u32[]{:S(2)}, u32[]{:S(2)}) collective-permute-start(bf16[4,2,64,2,256]{4,3,2,1,0:T(2,128)(2,1)S(1)} %all-to-all-done), channel_id=1, source_target_pairs={{0,2},{2,0},{4,6},{6,4},{1,3},{3,1},{5,7},{7,5},{8,10},{10,8},{12,... | collective-permute-start | bytes 1572872 | tf_op jit(solution)/shard_map/ppermute | solution.py:434
  21.0 0.1 pad_add_fusion.place_ref
  21.1 0.1 copy.8
  21.2 0.0 copy-start.4
  21.2 0.0 copy-done.1
  21.2 0.0 copy-done.2
  21.2 0.0 copy-done
  21.2 0.0 copy-start.3
  21.2 4.2 %shard_map.77 = (f32[8,2,8,256]{3,2,1,0:T(8,128)S(1)}, f32[8,2,128,256]{3,2,1,0:T(8,128)S(1)}) custom-call(s32[1,8]{1,0:T(1,128)S(1)} %copy-done.1, s32[1,8]{1,0:T(1,128)S(1)} %copy-done.2, s32[2]{0:T(128)S(1)} %pad_add_fusion.place_ref, bf16[256,2048]{1,0:T(8,128)(2,1)S(1)} %bitcast.35, bf16[512,512]{1,0:T(8,128)(2,1)S(1)} %bitcast.42), custom_call_target="tpu_custom_call" | custom-call | flops 1073741824 | bytes 2097152 | tf_op jit(solution)/shard_map/pallas_call | solution.py:356
  25.4 0.7 %collective-permute-start.2 = (bf16[256,2,256]{2,1,0:T(2,128)(2,1)S(1)}, bf16[256,2,256]{2,1,0:T(2,128)(2,1)S(1)}, u32[]{:S(2)}, u32[]{:S(2)}) collective-permute-start(bf16[256,2,256]{2,1,0:T(2,128)(2,1)S(1)} %collective-permute-done), channel_id=1, source_target_pairs={{2,4},{4,6},{3,5},{5,7},{10,12},{12,14},{11,13},{13,15},{18,20},{2... | collective-permute-start | bytes 786440 | tf_op jit(solution)/shard_map/ppermute | solution.py:437
  26.1 0.0 copy-done.4
  26.2 0.1 slice.9
  26.3 0.7 %collective-permute-start.3 = (bf16[128,2,256]{2,1,0:T(2,128)(2,1)S(1)}, bf16[128,2,256]{2,1,0:T(2,128)(2,1)S(1)}, u32[]{:S(2)}, u32[]{:S(2)}) collective-permute-start(bf16[128,2,256]{2,1,0:T(2,128)(2,1)S(1)} %slice.9), channel_id=1, source_target_pairs={{2,6},{3,7},{10,14},{11,15},{18,22},{19,23},{26,30},{27,31}} | collective-permute-start | bytes 393224 | tf_op jit(solution)/shard_map/ppermute | solution.py:438
  27.0 0.0 copy-done.3
  27.0 2.5 %shard_map.78 = (f32[8,2,8,256]{3,2,1,0:T(8,128)S(1)}, f32[8,2,128,256]{3,2,1,0:T(8,128)S(1)}) custom-call(s32[1,8]{1,0:T(1,128)S(1)} %copy-done.1, s32[2]{0:T(128)S(1)} %pad_add_fusion.place_ref, bf16[256,2048]{1,0:T(8,128)(2,1)S(1)} %bitcast.47, bf16[256,512]{1,0:T(8,128)(2,1)S(1)} %bitcast.43, bf16[256,512]{1,0:T(8,128)(2,1)S(1)} %bitcast.45), custom_call_target="tpu_custom_call" | custom-call | flops 2147483648 | bytes 2097152 | tf_op jit(solution)/shard_map/pallas_call | solution.py:356
  29.5 0.0 collective-permute-done.5
  29.5 1.1 %copy.16 = bf16[64,8,2,256]{3,1,2,0:T(8,128)(2,1)S(1)} copy(bf16[64,8,2,256]{3,2,1,0:T(2,128)(2,1)} %bitcast.29) | data formatting | bytes 1048576
  30.7 1.3 %collective-permute-start.9 = (bf16[512,512]{1,0:T(8,128)(2,1)S(1)}, bf16[512,512]{1,0:T(8,128)(2,1)S(1)}, u32[]{:S(2)}, u32[]{:S(2)}) collective-permute-start(bf16[512,512]{1,0:T(8,128)(2,1)S(1)} %bitcast.39), channel_id=1, source_target_pairs={{2,0},{4,6},{3,1},{5,7},{10,8},{12,14},{11,9},{13,15},{18,16},{20,... | collective-permute-start | bytes 1572872 | tf_op jit(solution)/shard_map/ppermute | solution.py:448
  32.0 0.0 collective-permute-done.3
  32.0 0.0 collective-permute-done.2
  32.0 0.0 collective-permute-done.1
  32.0 0.5 fusion
  32.5 0.7 %collective-permute-start.4 = (bf16[512,256]{1,0:T(8,128)(2,1)S(1)}, bf16[512,256]{1,0:T(8,128)(2,1)S(1)}, u32[]{:S(2)}, u32[]{:S(2)}) collective-permute-start(bf16[512,256]{1,0:T(8,128)(2,1)S(1)} %bitcast.59), channel_id=1, source_target_pairs={{2,4},{4,2},{3,5},{5,3},{10,12},{12,10},{11,13},{13,11},{18,20},{2... | collective-permute-start | bytes 786440 | tf_op jit(solution)/shard_map/ppermute | solution.py:450
  33.3 0.7 %collective-permute-start.7 = (bf16[512,256]{1,0:T(8,128)(2,1)S(1)}, bf16[512,256]{1,0:T(8,128)(2,1)S(1)}, u32[]{:S(2)}, u32[]{:S(2)}) collective-permute-start(bf16[512,256]{1,0:T(8,128)(2,1)S(1)} %bitcast.58), channel_id=1, source_target_pairs={{2,4},{4,2},{3,5},{5,3},{10,12},{12,10},{11,13},{13,11},{18,20},{2... | collective-permute-start | bytes 786440 | tf_op jit(solution)/shard_map/ppermute | solution.py:450
  34.0 0.1 copy.14
  34.0 4.3 %shard_map.80 = (f32[8,2,8,256]{3,2,1,0:T(8,128)S(1)}, f32[8,2,128,256]{3,2,1,0:T(8,128)S(1)}) custom-call(s32[1,8]{1,0:T(1,128)S(1)} %copy-done.1, s32[1,8]{1,0:T(1,128)S(1)} %copy-done.2, s32[2]{0:T(128)S(1)} %pad_add_fusion.place_ref, bf16[256,2048]{1,0:T(8,128)(2,1)S(1)} %bitcast.36, bf16[512,512]{1,0:T(8,128)(2,1)S(1)} %bitcast.41, ...), custom_call_target="tpu_custom_call" | custom-call | flops 1073741824 | bytes 2097152 | tf_op jit(solution)/shard_map/pallas_call | solution.py:356
  38.4 0.0 collective-permute-done.4.refs_0_
  38.4 1.3 %collective-permute-start.6 = (bf16[512,256]{1,0:T(8,128)(2,1)S(1)}, bf16[512,256]{1,0:T(8,128)(2,1)S(1)}, u32[]{:S(2)}, u32[]{:S(2)}) collective-permute-start(bf16[512,256]{1,0:T(8,128)(2,1)S(1)} %collective-permute-done.4.refs_0_), channel_id=1, source_target_pairs={{2,0},{4,6},{3,1},{5,7},{10,8},{12,14},{11,9},{13,15},{18,16},{20,... | collective-permute-start | bytes 786440 | tf_op jit(solution)/shard_map/ppermute | solution.py:458
  39.7 0.0 collective-permute-done.7.refs_2_
  39.7 1.3 %collective-permute-start.8 = (bf16[512,256]{1,0:T(8,128)(2,1)S(1)}, bf16[512,256]{1,0:T(8,128)(2,1)S(1)}, u32[]{:S(2)}, u32[]{:S(2)}) collective-permute-start(bf16[512,256]{1,0:T(8,128)(2,1)S(1)} %collective-permute-done.7.refs_2_), channel_id=1, source_target_pairs={{2,0},{4,6},{3,1},{5,7},{10,8},{12,14},{11,9},{13,15},{18,16},{20,... | collective-permute-start | bytes 786440 | tf_op jit(solution)/shard_map/ppermute | solution.py:458
  41.1 2.3 %shard_map.79 = bf16[256,2048]{1,0:T(8,128)(2,1)} custom-call(s32[1,8]{1,0:T(1,128)S(1)} %copy-done.1, s32[2]{0:T(128)S(1)} %pad_add_fusion.place_ref, bf16[256,2048]{1,0:T(8,128)(2,1)S(1)} %bitcast.48, bf16[256,512]{1,0:T(8,128)(2,1)S(1)} %bitcast.44, bf16[128,512]{1,0:T(8,128)(2,1)S(1)} %bitcast.46, f32[8,2,8,256]{3,2,1,0:T(8,128)S(1)} %get-tuple-element.35.refs_2_, ...), custom_call_target="tpu_custom_call" | custom-call | flops 1610612736 | bytes 2097152 | tf_op jit(solution)/shard_map/pallas_call | solution.py:356
  43.4 3.4 %collective-permute-done.9.refs_1_ = bf16[512,512]{1,0:T(8,128)(2,1)S(1)} collective-permute-done((bf16[512,512]{1,0:T(8,128)(2,1)S(1)}, bf16[512,512]{1,0:T(8,128)(2,1)S(1)}, u32[]{:S(2)}, u32[]{:S(2)}) %collective-permute-start.9) | collective-permute-done | bytes 524320 | tf_op jit(solution)/shard_map/ppermute | solution.py:448
  46.8 4.4 %shard_map.81 = (f32[8,2,8,256]{3,2,1,0:T(8,128)S(1)}, f32[8,2,128,256]{3,2,1,0:T(8,128)S(1)}) custom-call(s32[1,8]{1,0:T(1,128)S(1)} %copy-done.1, s32[1,8]{1,0:T(1,128)S(1)} %copy-done.2, s32[2]{0:T(128)S(1)} %pad_add_fusion.place_ref, bf16[256,2048]{1,0:T(8,128)(2,1)S(1)} %bitcast.37, bf16[512,512]{1,0:T(8,128)(2,1)S(1)} %bitcast.40, ...), custom_call_target="tpu_custom_call" | custom-call | flops 1073741824 | bytes 2097152 | tf_op jit(solution)/shard_map/pallas_call | solution.py:356
  51.2 6.5 %collective-permute-done.6.refs_1_ = bf16[512,256]{1,0:T(8,128)(2,1)S(1)} collective-permute-done((bf16[512,256]{1,0:T(8,128)(2,1)S(1)}, bf16[512,256]{1,0:T(8,128)(2,1)S(1)}, u32[]{:S(2)}, u32[]{:S(2)}) %collective-permute-start.6) | collective-permute-done | bytes 262176 | tf_op jit(solution)/shard_map/ppermute | solution.py:458
  57.6 2.8 %collective-permute-done.8.refs_3_ = bf16[512,256]{1,0:T(8,128)(2,1)S(1)} collective-permute-done((bf16[512,256]{1,0:T(8,128)(2,1)S(1)}, bf16[512,256]{1,0:T(8,128)(2,1)S(1)}, u32[]{:S(2)}, u32[]{:S(2)}) %collective-permute-start.8) | collective-permute-done | bytes 262176 | tf_op jit(solution)/shard_map/ppermute | solution.py:458
  60.5 5.6 %shard_map.82 = bf16[256,2048]{1,0:T(8,128)(2,1)} custom-call(s32[1,8]{1,0:T(1,128)S(1)} %copy-done.1, s32[1,8]{1,0:T(1,128)S(1)} %copy-done.2, s32[2]{0:T(128)S(1)} %pad_add_fusion.place_ref, bf16[256,2048]{1,0:T(8,128)(2,1)S(1)} %bitcast.38, bf16[512,256]{1,0:T(8,128)(2,1)S(1)} %collective-permute-done.4.refs_0_, ...), custom_call_target="tpu_custom_call" | custom-call | flops 1073741824 | bytes 2097152 | tf_op jit(solution)/shard_map/pallas_call | solution.py:356
  (6 shorter events, 0.2 us)
Async XLA Ops:
  0.6 20.6 %copy-start.1 = (s32[1,8]{1,0:T(1,128)S(1)}, s32[1,8]{1,0:T(1,128)}, u32[]{:S(2)}) copy-start(s32[1,8]{1,0:T(1,128)} %lengths_ref.11) | copy-start | bytes 100
  0.6 20.6 %copy-start.2 = (s32[1,8]{1,0:T(1,128)S(1)}, s32[1,8]{1,0:T(1,128)}, u32[]{:S(2)}) copy-start(s32[1,8]{1,0:T(1,128)} %images_ref.7) | copy-start | bytes 100
  0.7 20.6 %copy-start = (bf16[1,256,2048]{2,1,0:T(8,128)(2,1)S(1)}, bf16[1,256,2048]{2,1,0:T(8,128)(2,1)}, u32[]{:S(2)}) copy-start(bf16[1,256,2048]{2,1,0:T(8,128)(2,1)} %param.8) | copy-start | bytes 3145732
  0.7 14.4 %all-to-all-start = ((bf16[4,2,64,2,256]{4,3,2,1,0:T(2,128)(2,1)}), bf16[4,2,64,2,256]{4,3,2,1,0:T(2,128)(2,1)S(1)}, u32[]{:S(2)}, u32[]{:S(2)}) async-start(bf16[4,2,64,2,256]{4,3,2,1,0:T(2,128)(2,1)} %param.9), calls=%async_computation | async-start | bytes 1048576 | tf_op jit(solution)/shard_map/all_to_all | solution.py:417
  6.0 9.1 %collective-permute-start = (bf16[256,2,256]{2,1,0:T(2,128)(2,1)}, bf16[256,2,256]{2,1,0:T(2,128)(2,1)S(1)}, u32[]{:S(2)}, u32[]{:S(2)}) collective-permute-start(bf16[256,2,256]{2,1,0:T(2,128)(2,1)} %bitcast.55), channel_id=1, source_target_pairs={{0,2},{2,4},{4,6},{1,3},{3,5},{5,7},{8,10},{10,12},{12,14},{9,11},... | collective-permute-start | bytes 786440 | tf_op jit(solution)/shard_map/ppermute | solution.py:413
  15.1 14.4 %collective-permute-start.5 = (bf16[4,2,64,2,256]{4,3,2,1,0:T(2,128)(2,1)S(1)}, bf16[4,2,64,2,256]{4,3,2,1,0:T(2,128)(2,1)}, u32[]{:S(2)}, u32[]{:S(2)}) collective-permute-start(bf16[4,2,64,2,256]{4,3,2,1,0:T(2,128)(2,1)S(1)} %all-to-all-done), channel_id=1, source_target_pairs={{2,4},{4,2},{3,5},{5,3},{10,12},{12,10},{11,13},{13,11},{18,20},{2... | collective-permute-start | bytes 1572872 | tf_op jit(solution)/shard_map/ppermute | solution.py:433
  16.5 15.4 %collective-permute-start.1 = (bf16[4,2,64,2,256]{4,3,2,1,0:T(2,128)(2,1)S(1)}, bf16[4,2,64,2,256]{4,3,2,1,0:T(2,128)(2,1)S(1)}, u32[]{:S(2)}, u32[]{:S(2)}) collective-permute-start(bf16[4,2,64,2,256]{4,3,2,1,0:T(2,128)(2,1)S(1)} %all-to-all-done), channel_id=1, source_target_pairs={{0,2},{2,0},{4,6},{6,4},{1,3},{3,1},{5,7},{7,5},{8,10},{10,8},{12,... | collective-permute-start | bytes 1572872 | tf_op jit(solution)/shard_map/ppermute | solution.py:434
  21.2 4.9 %copy-start.4 = (bf16[1,256,2,256]{3,2,1,0:T(2,128)(2,1)S(1)}, bf16[1,256,2,256]{3,2,1,0:T(2,128)(2,1)}, u32[]{:S(2)}) copy-start(bf16[1,256,2,256]{3,2,1,0:T(2,128)(2,1)} %param.7) | copy-start | bytes 786436
  21.2 5.8 %copy-start.3 = (bf16[1,256,2048]{2,1,0:T(8,128)(2,1)S(1)}, bf16[1,256,2048]{2,1,0:T(8,128)(2,1)}, u32[]{:S(2)}) copy-start(bf16[1,256,2048]{2,1,0:T(8,128)(2,1)} %param.6) | copy-start | bytes 3145732
  25.4 6.6 %collective-permute-start.2 = (bf16[256,2,256]{2,1,0:T(2,128)(2,1)S(1)}, bf16[256,2,256]{2,1,0:T(2,128)(2,1)S(1)}, u32[]{:S(2)}, u32[]{:S(2)}) collective-permute-start(bf16[256,2,256]{2,1,0:T(2,128)(2,1)S(1)} %collective-permute-done), channel_id=1, source_target_pairs={{2,4},{4,6},{3,5},{5,7},{10,12},{12,14},{11,13},{13,15},{18,20},{2... | collective-permute-start | bytes 786440 | tf_op jit(solution)/shard_map/ppermute | solution.py:437
  26.3 5.7 %collective-permute-start.3 = (bf16[128,2,256]{2,1,0:T(2,128)(2,1)S(1)}, bf16[128,2,256]{2,1,0:T(2,128)(2,1)S(1)}, u32[]{:S(2)}, u32[]{:S(2)}) collective-permute-start(bf16[128,2,256]{2,1,0:T(2,128)(2,1)S(1)} %slice.9), channel_id=1, source_target_pairs={{2,6},{3,7},{10,14},{11,15},{18,22},{19,23},{26,30},{27,31}} | collective-permute-start | bytes 393224 | tf_op jit(solution)/shard_map/ppermute | solution.py:438
  30.7 16.1 %collective-permute-start.9 = (bf16[512,512]{1,0:T(8,128)(2,1)S(1)}, bf16[512,512]{1,0:T(8,128)(2,1)S(1)}, u32[]{:S(2)}, u32[]{:S(2)}) collective-permute-start(bf16[512,512]{1,0:T(8,128)(2,1)S(1)} %bitcast.39), channel_id=1, source_target_pairs={{2,0},{4,6},{3,1},{5,7},{10,8},{12,14},{11,9},{13,15},{18,16},{20,... | collective-permute-start | bytes 1572872 | tf_op jit(solution)/shard_map/ppermute | solution.py:448
  32.5 5.8 %collective-permute-start.4 = (bf16[512,256]{1,0:T(8,128)(2,1)S(1)}, bf16[512,256]{1,0:T(8,128)(2,1)S(1)}, u32[]{:S(2)}, u32[]{:S(2)}) collective-permute-start(bf16[512,256]{1,0:T(8,128)(2,1)S(1)} %bitcast.59), channel_id=1, source_target_pairs={{2,4},{4,2},{3,5},{5,3},{10,12},{12,10},{11,13},{13,11},{18,20},{2... | collective-permute-start | bytes 786440 | tf_op jit(solution)/shard_map/ppermute | solution.py:450
  33.3 6.4 %collective-permute-start.7 = (bf16[512,256]{1,0:T(8,128)(2,1)S(1)}, bf16[512,256]{1,0:T(8,128)(2,1)S(1)}, u32[]{:S(2)}, u32[]{:S(2)}) collective-permute-start(bf16[512,256]{1,0:T(8,128)(2,1)S(1)} %bitcast.58), channel_id=1, source_target_pairs={{2,4},{4,2},{3,5},{5,3},{10,12},{12,10},{11,13},{13,11},{18,20},{2... | collective-permute-start | bytes 786440 | tf_op jit(solution)/shard_map/ppermute | solution.py:450
  38.4 19.3 %collective-permute-start.6 = (bf16[512,256]{1,0:T(8,128)(2,1)S(1)}, bf16[512,256]{1,0:T(8,128)(2,1)S(1)}, u32[]{:S(2)}, u32[]{:S(2)}) collective-permute-start(bf16[512,256]{1,0:T(8,128)(2,1)S(1)} %collective-permute-done.4.refs_0_), channel_id=1, source_target_pairs={{2,0},{4,6},{3,1},{5,7},{10,8},{12,14},{11,9},{13,15},{18,16},{20,... | collective-permute-start | bytes 786440 | tf_op jit(solution)/shard_map/ppermute | solution.py:458
  39.7 20.8 %collective-permute-start.8 = (bf16[512,256]{1,0:T(8,128)(2,1)S(1)}, bf16[512,256]{1,0:T(8,128)(2,1)S(1)}, u32[]{:S(2)}, u32[]{:S(2)}) collective-permute-start(bf16[512,256]{1,0:T(8,128)(2,1)S(1)} %collective-permute-done.7.refs_2_), channel_id=1, source_target_pairs={{2,0},{4,6},{3,1},{5,7},{10,8},{12,14},{11,9},{13,15},{18,16},{20,... | collective-permute-start | bytes 786440 | tf_op jit(solution)/shard_map/ppermute | solution.py:458
where the time goes:
time: 67.1 us; the launch traced here: 66.2 us
  Pallas kernels  23.3 us (35%)
  starting transfers between devices  21.3 us (32%)
  waiting for transfers between devices  18.4 us (27%)
  local copies, waits for them, and re-layouts  2.08 us (3%)
  between operations  1.1 us (2%)
    pallas_call x6, Pallas kernels, state_call(): pl.pallas_call(kernel, out_shape=out_shape, in_specs=in_specs, out_specs=...  23.3 us
    ppermute x2, waiting for transfers between devices, per_device(): far_on = [lax.ppermute(part, 'ctx', [(1, 0), (2, 3)]) for part in far]  9.29 us
    ppermute x1, waiting for transfers between devices, per_device(): lax.ppermute(piece, 'ctx', [(c, c + 1) for c in range(step - 1, n_ctx - 1)])  5.62 us
    all_to_all x1, starting transfers between devices, per_device(): lax.all_to_all(kv_cross, 'pipe', split_axis=0, concat_axis=0, tiled=True)  5.31 us
    ppermute x1, starting transfers between devices, per_device(): pair = lax.ppermute(arrived, 'ctx', [(0, 1), (1, 0), (2, 3), (3, 2)])  4.46 us
    ppermute x1, starting transfers between devices, per_device(): lax.ppermute(piece, 'ctx', [(c, c + 1) for c in range(step - 1, n_ctx - 1)])  3.49 us
    ppermute x1, waiting for transfers between devices, per_device(): near_on = lax.ppermute(near, 'ctx', [(1, 0), (2, 3)])  3.42 us
    ppermute x2, starting transfers between devices, per_device(): far_on = [lax.ppermute(part, 'ctx', [(1, 0), (2, 3)]) for part in far]  2.58 us
  transfers between devices with their start and end apart: 11, of which 4 were waited for; matrix products, arithmetic and copies ran while one was open for 3% of the time, Pallas kernels for 27%

commit v1 on v0

--- a/solution.py
+++ b/solution.py
@@ -440,8 +440,9 @@
         parts = ((0, 0, 0, 0, rows, None), (1, 1, 0, 0, rows, None))
         self_state = attend_self([own, flat(passed)], early, parts, None, False)
         near, state = lax.optimization_barrier((near, state))
-        pair, two_back, three_back, self_state = lax.optimization_barrier(
-            (pair, two_back, three_back, self_state)
+        state = attend_cross([[at(flat(pair))]], state, False)
+        pair, two_back, three_back, self_state, state = lax.optimization_barrier(
+            (pair, two_back, three_back, self_state, state)
         )
 
         near = flat(near)
@@ -450,11 +451,10 @@
             lax.ppermute(flat(pair[..., g * HD : (g + 1) * HD]), "ctx", [(1, 2), (2, 1)])
             for g in range(kv_heads)
         ]
-        state = attend_cross([[at(flat(pair))]], state, False)
-        far[0], state = lax.optimization_barrier((far[0], state))
         late = ((2, rows), (3, half))
         parts = ((0, 0, 0, 0, rows, None), (1, 1, 0, 0, half, 3))
         self_out = attend_self([flat(two_back), flat(three_back)], late, parts, self_state, True)
+        far[-1], self_out = lax.optimization_barrier((far[-1], self_out))
         far_on = [lax.ppermute(part, "ctx", [(1, 0), (2, 3)]) for part in far]
         state = attend_cross([[at(near), at(near_on)]], state, False)
         last = [[at(far[g], g), at(far_on[g], g)] for g in range(kv_heads)]

time: 67.1 us -> 71.4 us (1.064)
  waiting for transfers between devices: 18.4 us -> 26 us
  starting transfers between devices: 21.3 us -> 19.2 us
  Pallas kernels: 23.3 us -> 21.3 us
  local copies, waits for them, and re-layouts: 2.08 us -> 3.02 us
    ppermute x1, waiting for transfers between devices: 3.42 us -> 8.06 us  [per_device(): near_on = lax.ppermute(near, 'ctx', [(1, 0), (2, 3)])]
    ppermute x2, waiting for transfers between devices: 9.29 us -> 11.9 us  [per_device(): far_on = [lax.ppermute(part, 'ctx', [(1, 0), (2, 3)]) for part in far]]
    ppermute x1, starting transfers between devices: 4.46 us -> 2.38 us  [per_device(): pair = lax.ppermute(arrived, 'ctx', [(0, 1), (1, 0), (2, 3), (3, 2)])]
    pallas_call x6, Pallas kernels: 23.3 us -> 21.3 us  [state_call(): pl.pallas_call(kernel, out_shape=out_shape, in_specs=in_specs, out_specs=...]
    unnamed x19 -> x17, local copies, waits for them, and re-layouts: 1.51 us -> 2.45 us
  transfers between devices with their start and end apart: 11 -> 11, of which waited for: 4 -> 5; matrix products, arithmetic and copies ran while one was open for 3% -> 4% of each run, Pallas kernels for 27% -> 23%
where the time goes in v1:
time: 71.4 us; the launch traced here: 70.7 us
  waiting for transfers between devices  26 us (36%)
  Pallas kernels  21.3 us (30%)
  starting transfers between devices  19.2 us (27%)
  local copies, waits for them, and re-layouts  3.02 us (4%)
  between operations  1.07 us (1%)
    pallas_call x6, Pallas kernels, state_call(): pl.pallas_call(kernel, out_shape=out_shape, in_specs=in_specs, out_specs=...  21.3 us
    ppermute x2, waiting for transfers between devices, per_device(): far_on = [lax.ppermute(part, 'ctx', [(1, 0), (2, 3)]) for part in far]  11.9 us
    ppermute x1, waiting for transfers between devices, per_device(): near_on = lax.ppermute(near, 'ctx', [(1, 0), (2, 3)])  8.06 us
    ppermute x1, waiting for transfers between devices, per_device(): lax.ppermute(piece, 'ctx', [(c, c + 1) for c in range(step - 1, n_ctx - 1)])  5.62 us
    all_to_all x1, starting transfers between devices, per_device(): lax.all_to_all(kv_cross, 'pipe', split_axis=0, concat_axis=0, tiled=True)  5.31 us
    ppermute x1, starting transfers between devices, per_device(): lax.ppermute(piece, 'ctx', [(c, c + 1) for c in range(step - 1, n_ctx - 1)])  3.48 us
    ppermute x2, starting transfers between devices, per_device(): far_on = [lax.ppermute(part, 'ctx', [(1, 0), (2, 3)]) for part in far]  2.57 us
    unnamed x17, local copies, waits for them, and re-layouts  2.45 us
  transfers between devices with their start and end apart: 11, of which 5 were waited for; matrix products, arithmetic and copies ran while one was open for 4% of the time, Pallas kernels for 23%

profile of v1, /device:TPU:0, one launch (start us, length us, event | category | flops | bytes accessed | tf_op | source)
XLA Modules:
  0.0 70.7 jit_solution(9076262951852033164)
XLA Ops:
  0.6 0.0 copy-start.1
  0.6 0.0 copy-start.2
  0.7 0.0 copy-start
  0.7 5.3 %all-to-all-start = ((bf16[4,2,64,2,256]{4,3,2,1,0:T(2,128)(2,1)}), bf16[4,2,64,2,256]{4,3,2,1,0:T(2,128)(2,1)S(1)}, u32[]{:S(2)}, u32[]{:S(2)}) async-start(bf16[4,2,64,2,256]{4,3,2,1,0:T(2,128)(2,1)} %param.9), calls=%async_computation | async-start | bytes 1048576 | tf_op jit(solution)/shard_map/all_to_all | solution.py:417
  6.0 3.5 %collective-permute-start = (bf16[256,2,256]{2,1,0:T(2,128)(2,1)}, bf16[256,2,256]{2,1,0:T(2,128)(2,1)S(1)}, u32[]{:S(2)}, u32[]{:S(2)}) collective-permute-start(bf16[256,2,256]{2,1,0:T(2,128)(2,1)} %bitcast.55), channel_id=1, source_target_pairs={{0,2},{2,4},{4,6},{1,3},{3,5},{5,7},{8,10},{10,12},{12,14},{9,11},... | collective-permute-start | bytes 786440 | tf_op jit(solution)/shard_map/ppermute | solution.py:413
  9.5 5.6 %collective-permute-done = bf16[256,2,256]{2,1,0:T(2,128)(2,1)S(1)} collective-permute-done((bf16[256,2,256]{2,1,0:T(2,128)(2,1)}, bf16[256,2,256]{2,1,0:T(2,128)(2,1)S(1)}, u32[]{:S(2)}, u32[]{:S(2)}) %collective-permute-start) | collective-permute-done | bytes 262176 | tf_op jit(solution)/shard_map/ppermute | solution.py:413
  15.1 0.0 all-to-all-done
  15.1 2.4 %collective-permute-start.1 = (bf16[4,2,64,2,256]{4,3,2,1,0:T(2,128)(2,1)S(1)}, bf16[4,2,64,2,256]{4,3,2,1,0:T(2,128)(2,1)S(1)}, u32[]{:S(2)}, u32[]{:S(2)}) collective-permute-start(bf16[4,2,64,2,256]{4,3,2,1,0:T(2,128)(2,1)S(1)} %all-to-all-done), channel_id=1, source_target_pairs={{0,2},{2,0},{4,6},{6,4},{1,3},{3,1},{5,7},{7,5},{8,10},{10,8},{12,... | collective-permute-start | bytes 1572872 | tf_op jit(solution)/shard_map/ppermute | solution.py:434
  17.5 1.4 %collective-permute-start.4 = (bf16[4,2,64,2,256]{4,3,2,1,0:T(2,128)(2,1)S(1)}, bf16[4,2,64,2,256]{4,3,2,1,0:T(2,128)(2,1)}, u32[]{:S(2)}, u32[]{:S(2)}) collective-permute-start(bf16[4,2,64,2,256]{4,3,2,1,0:T(2,128)(2,1)S(1)} %all-to-all-done), channel_id=1, source_target_pairs={{2,4},{4,2},{3,5},{5,3},{10,12},{12,10},{11,13},{13,11},{18,20},{2... | collective-permute-start | bytes 1572872 | tf_op jit(solution)/shard_map/ppermute | solution.py:433
  18.9 1.0 %copy.9 = bf16[32,8,2,256]{3,1,2,0:T(8,128)(2,1)S(1)} copy(bf16[32,8,2,256]{3,2,1,0:T(2,128)(2,1)} %bitcast.56) | data formatting | bytes 524288
  19.9 0.1 pad_add_fusion.place_ref
  20.0 0.1 copy.8
  20.1 0.0 copy-done.1
  20.1 0.0 copy-done.2
  20.1 0.0 copy-done
  20.1 0.0 copy-start.3
  20.1 3.7 %shard_map.77 = (f32[8,2,8,256]{3,2,1,0:T(8,128)S(1)}, f32[8,2,128,256]{3,2,1,0:T(8,128)S(1)}) custom-call(s32[1,8]{1,0:T(1,128)S(1)} %copy-done.1, s32[1,8]{1,0:T(1,128)S(1)} %copy-done.2, s32[2]{0:T(128)S(1)} %pad_add_fusion.place_ref, bf16[256,2048]{1,0:T(8,128)(2,1)S(1)} %bitcast.35, bf16[512,512]{1,0:T(8,128)(2,1)S(1)} %bitcast.42), custom_call_target="tpu_custom_call" | custom-call | flops 1073741824 | bytes 2097152 | tf_op jit(solution)/shard_map/pallas_call | solution.py:356
  23.8 0.1 slice.9
  23.9 0.7 collective-permute-start.2
  24.6 0.7 collective-permute-start.3
  25.3 0.0 copy-done.3
  25.3 2.5 %shard_map.78 = (f32[8,2,8,256]{3,2,1,0:T(8,128)S(1)}, f32[8,2,128,256]{3,2,1,0:T(8,128)S(1)}) custom-call(s32[1,8]{1,0:T(1,128)S(1)} %copy-done.1, s32[2]{0:T(128)S(1)} %pad_add_fusion.place_ref, bf16[256,2048]{1,0:T(8,128)(2,1)S(1)} %bitcast.47, bf16[256,512]{1,0:T(8,128)(2,1)S(1)} %bitcast.43, bf16[256,512]{1,0:T(8,128)(2,1)S(1)} %bitcast.45), custom_call_target="tpu_custom_call" | custom-call | flops 2147483648 | bytes 2097152 | tf_op jit(solution)/shard_map/pallas_call | solution.py:356
  27.9 0.4 collective-permute-done.1
  28.2 0.1 copy.11
  28.3 0.0 collective-permute-done.4
  28.3 1.1 %copy.16 = bf16[64,8,2,256]{3,1,2,0:T(8,128)(2,1)S(1)} copy(bf16[64,8,2,256]{3,2,1,0:T(2,128)(2,1)} %bitcast.29) | data formatting | bytes 1048576
  29.5 1.3 %collective-permute-start.9 = (bf16[512,512]{1,0:T(8,128)(2,1)S(1)}, bf16[512,512]{1,0:T(8,128)(2,1)S(1)}, u32[]{:S(2)}, u32[]{:S(2)}) collective-permute-start(bf16[512,512]{1,0:T(8,128)(2,1)S(1)} %bitcast.39), channel_id=1, source_target_pairs={{2,0},{4,6},{3,1},{5,7},{10,8},{12,14},{11,9},{13,15},{18,16},{20,... | collective-permute-start | bytes 1572872 | tf_op jit(solution)/shard_map/ppermute | solution.py:449
  30.8 3.8 %shard_map.79 = (f32[8,2,8,256]{3,2,1,0:T(8,128)S(1)}, f32[8,2,128,256]{3,2,1,0:T(8,128)S(1)}) custom-call(s32[1,8]{1,0:T(1,128)S(1)} %copy-done.1, s32[1,8]{1,0:T(1,128)S(1)} %copy-done.2, s32[2]{0:T(128)S(1)} %pad_add_fusion.place_ref, bf16[256,2048]{1,0:T(8,128)(2,1)S(1)} %bitcast.36, bf16[512,512]{1,0:T(8,128)(2,1)S(1)} %bitcast.41, ...), custom_call_target="tpu_custom_call" | custom-call | flops 1073741824 | bytes 2097152 | tf_op jit(solution)/shard_map/pallas_call | solution.py:356
  34.6 0.0 collective-permute-done.3
  34.6 0.0 collective-permute-done.2
  34.6 0.5 fusion
  35.2 0.7 collective-permute-start.5
  35.9 0.7 collective-permute-start.6
  36.6 2.3 %shard_map.80 = bf16[256,2048]{1,0:T(8,128)(2,1)} custom-call(s32[1,8]{1,0:T(1,128)S(1)} %copy-done.1, s32[2]{0:T(128)S(1)} %pad_add_fusion.place_ref, bf16[256,2048]{1,0:T(8,128)(2,1)S(1)} %bitcast.48, bf16[256,512]{1,0:T(8,128)(2,1)S(1)} %bitcast.44, bf16[128,512]{1,0:T(8,128)(2,1)S(1)} %bitcast.46, f32[8,2,8,256]{3,2,1,0:T(8,128)S(1)} %get-tuple-element.43.refs_2_, ...), custom_call_target="tpu_custom_call" | custom-call | flops 1610612736 | bytes 2097152 | tf_op jit(solution)/shard_map/pallas_call | solution.py:356
  38.9 0.0 collective-permute-done.5.refs_2_
  38.9 1.3 %collective-permute-start.8 = (bf16[512,256]{1,0:T(8,128)(2,1)S(1)}, bf16[512,256]{1,0:T(8,128)(2,1)S(1)}, u32[]{:S(2)}, u32[]{:S(2)}) collective-permute-start(bf16[512,256]{1,0:T(8,128)(2,1)S(1)} %collective-permute-done.5.refs_2_), channel_id=1, source_target_pairs={{2,0},{4,6},{3,1},{5,7},{10,8},{12,14},{11,9},{13,15},{18,16},{20,... | collective-permute-start | bytes 786440 | tf_op jit(solution)/shard_map/ppermute | solution.py:458
  40.2 0.0 collective-permute-done.6.refs_0_
  40.2 1.3 %collective-permute-start.7 = (bf16[512,256]{1,0:T(8,128)(2,1)S(1)}, bf16[512,256]{1,0:T(8,128)(2,1)S(1)}, u32[]{:S(2)}, u32[]{:S(2)}) collective-permute-start(bf16[512,256]{1,0:T(8,128)(2,1)S(1)} %collective-permute-done.6.refs_0_), channel_id=1, source_target_pairs={{2,0},{4,6},{3,1},{5,7},{10,8},{12,14},{11,9},{13,15},{18,16},{20,... | collective-permute-start | bytes 786440 | tf_op jit(solution)/shard_map/ppermute | solution.py:458
  41.5 8.1 %collective-permute-done.9.refs_1_ = bf16[512,512]{1,0:T(8,128)(2,1)S(1)} collective-permute-done((bf16[512,512]{1,0:T(8,128)(2,1)S(1)}, bf16[512,512]{1,0:T(8,128)(2,1)S(1)}, u32[]{:S(2)}, u32[]{:S(2)}) %collective-permute-start.9) | collective-permute-done | bytes 524320 | tf_op jit(solution)/shard_map/ppermute | solution.py:449
  49.6 3.9 %shard_map.81 = (f32[8,2,8,256]{3,2,1,0:T(8,128)S(1)}, f32[8,2,128,256]{3,2,1,0:T(8,128)S(1)}) custom-call(s32[1,8]{1,0:T(1,128)S(1)} %copy-done.1, s32[1,8]{1,0:T(1,128)S(1)} %copy-done.2, s32[2]{0:T(128)S(1)} %pad_add_fusion.place_ref, bf16[256,2048]{1,0:T(8,128)(2,1)S(1)} %bitcast.37, bf16[512,512]{1,0:T(8,128)(2,1)S(1)} %bitcast.40, ...), custom_call_target="tpu_custom_call" | custom-call | flops 1073741824 | bytes 2097152 | tf_op jit(solution)/shard_map/pallas_call | solution.py:356
  53.5 9.1 %collective-permute-done.8.refs_3_ = bf16[512,256]{1,0:T(8,128)(2,1)S(1)} collective-permute-done((bf16[512,256]{1,0:T(8,128)(2,1)S(1)}, bf16[512,256]{1,0:T(8,128)(2,1)S(1)}, u32[]{:S(2)}, u32[]{:S(2)}) %collective-permute-start.8) | collective-permute-done | bytes 262176 | tf_op jit(solution)/shard_map/ppermute | solution.py:458
  62.6 2.8 %collective-permute-done.7.refs_1_ = bf16[512,256]{1,0:T(8,128)(2,1)S(1)} collective-permute-done((bf16[512,256]{1,0:T(8,128)(2,1)S(1)}, bf16[512,256]{1,0:T(8,128)(2,1)S(1)}, u32[]{:S(2)}, u32[]{:S(2)}) %collective-permute-start.7) | collective-permute-done | bytes 262176 | tf_op jit(solution)/shard_map/ppermute | solution.py:458
  65.4 5.1 %shard_map.82 = bf16[256,2048]{1,0:T(8,128)(2,1)} custom-call(s32[1,8]{1,0:T(1,128)S(1)} %copy-done.1, s32[1,8]{1,0:T(1,128)S(1)} %copy-done.2, s32[2]{0:T(128)S(1)} %pad_add_fusion.place_ref, bf16[256,2048]{1,0:T(8,128)(2,1)S(1)} %bitcast.38, bf16[512,256]{1,0:T(8,128)(2,1)S(1)} %collective-permute-done.6.refs_0_, ...), custom_call_target="tpu_custom_call" | custom-call | flops 1073741824 | bytes 2097152 | tf_op jit(solution)/shard_map/pallas_call | solution.py:356
  (5 shorter events, 0.2 us)
Async XLA Ops:
  0.6 19.4 %copy-start.1 = (s32[1,8]{1,0:T(1,128)S(1)}, s32[1,8]{1,0:T(1,128)}, u32[]{:S(2)}) copy-start(s32[1,8]{1,0:T(1,128)} %lengths_ref.11) | copy-start | bytes 100
  0.6 19.4 %copy-start.2 = (s32[1,8]{1,0:T(1,128)S(1)}, s32[1,8]{1,0:T(1,128)}, u32[]{:S(2)}) copy-start(s32[1,8]{1,0:T(1,128)} %images_ref.7) | copy-start | bytes 100
  0.7 19.4 %copy-start = (bf16[1,256,2048]{2,1,0:T(8,128)(2,1)S(1)}, bf16[1,256,2048]{2,1,0:T(8,128)(2,1)}, u32[]{:S(2)}) copy-start(bf16[1,256,2048]{2,1,0:T(8,128)(2,1)} %param.8) | copy-start | bytes 3145732
  0.7 14.4 %all-to-all-start = ((bf16[4,2,64,2,256]{4,3,2,1,0:T(2,128)(2,1)}), bf16[4,2,64,2,256]{4,3,2,1,0:T(2,128)(2,1)S(1)}, u32[]{:S(2)}, u32[]{:S(2)}) async-start(bf16[4,2,64,2,256]{4,3,2,1,0:T(2,128)(2,1)} %param.9), calls=%async_computation | async-start | bytes 1048576 | tf_op jit(solution)/shard_map/all_to_all | solution.py:417
  6.0 9.1 %collective-permute-start = (bf16[256,2,256]{2,1,0:T(2,128)(2,1)}, bf16[256,2,256]{2,1,0:T(2,128)(2,1)S(1)}, u32[]{:S(2)}, u32[]{:S(2)}) collective-permute-start(bf16[256,2,256]{2,1,0:T(2,128)(2,1)} %bitcast.55), channel_id=1, source_target_pairs={{0,2},{2,4},{4,6},{1,3},{3,5},{5,7},{8,10},{10,12},{12,14},{9,11},... | collective-permute-start | bytes 786440 | tf_op jit(solution)/shard_map/ppermute | solution.py:413
  15.1 13.2 %collective-permute-start.1 = (bf16[4,2,64,2,256]{4,3,2,1,0:T(2,128)(2,1)S(1)}, bf16[4,2,64,2,256]{4,3,2,1,0:T(2,128)(2,1)S(1)}, u32[]{:S(2)}, u32[]{:S(2)}) collective-permute-start(bf16[4,2,64,2,256]{4,3,2,1,0:T(2,128)(2,1)S(1)} %all-to-all-done), channel_id=1, source_target_pairs={{0,2},{2,0},{4,6},{6,4},{1,3},{3,1},{5,7},{7,5},{8,10},{10,8},{12,... | collective-permute-start | bytes 1572872 | tf_op jit(solution)/shard_map/ppermute | solution.py:434
  17.5 10.9 %collective-permute-start.4 = (bf16[4,2,64,2,256]{4,3,2,1,0:T(2,128)(2,1)S(1)}, bf16[4,2,64,2,256]{4,3,2,1,0:T(2,128)(2,1)}, u32[]{:S(2)}, u32[]{:S(2)}) collective-permute-start(bf16[4,2,64,2,256]{4,3,2,1,0:T(2,128)(2,1)S(1)} %all-to-all-done), channel_id=1, source_target_pairs={{2,4},{4,2},{3,5},{5,3},{10,12},{12,10},{11,13},{13,11},{18,20},{2... | collective-permute-start | bytes 1572872 | tf_op jit(solution)/shard_map/ppermute | solution.py:433
  20.1 5.2 %copy-start.3 = (bf16[1,256,2048]{2,1,0:T(8,128)(2,1)S(1)}, bf16[1,256,2048]{2,1,0:T(8,128)(2,1)}, u32[]{:S(2)}) copy-start(bf16[1,256,2048]{2,1,0:T(8,128)(2,1)} %param.6) | copy-start | bytes 3145732
  23.9 10.7 %collective-permute-start.2 = (bf16[256,2,256]{2,1,0:T(2,128)(2,1)S(1)}, bf16[256,2,256]{2,1,0:T(2,128)(2,1)S(1)}, u32[]{:S(2)}, u32[]{:S(2)}) collective-permute-start(bf16[256,2,256]{2,1,0:T(2,128)(2,1)S(1)} %collective-permute-done), channel_id=1, source_target_pairs={{2,4},{4,6},{3,5},{5,7},{10,12},{12,14},{11,13},{13,15},{18,20},{2... | collective-permute-start | bytes 786440 | tf_op jit(solution)/shard_map/ppermute | solution.py:437
  24.6 10.0 %collective-permute-start.3 = (bf16[128,2,256]{2,1,0:T(2,128)(2,1)S(1)}, bf16[128,2,256]{2,1,0:T(2,128)(2,1)S(1)}, u32[]{:S(2)}, u32[]{:S(2)}) collective-permute-start(bf16[128,2,256]{2,1,0:T(2,128)(2,1)S(1)} %slice.9), channel_id=1, source_target_pairs={{2,6},{3,7},{10,14},{11,15},{18,22},{19,23},{26,30},{27,31}} | collective-permute-start | bytes 393224 | tf_op jit(solution)/shard_map/ppermute | solution.py:438
  29.5 20.1 %collective-permute-start.9 = (bf16[512,512]{1,0:T(8,128)(2,1)S(1)}, bf16[512,512]{1,0:T(8,128)(2,1)S(1)}, u32[]{:S(2)}, u32[]{:S(2)}) collective-permute-start(bf16[512,512]{1,0:T(8,128)(2,1)S(1)} %bitcast.39), channel_id=1, source_target_pairs={{2,0},{4,6},{3,1},{5,7},{10,8},{12,14},{11,9},{13,15},{18,16},{20,... | collective-permute-start | bytes 1572872 | tf_op jit(solution)/shard_map/ppermute | solution.py:449
  35.2 3.8 %collective-permute-start.5 = (bf16[512,256]{1,0:T(8,128)(2,1)S(1)}, bf16[512,256]{1,0:T(8,128)(2,1)S(1)}, u32[]{:S(2)}, u32[]{:S(2)}) collective-permute-start(bf16[512,256]{1,0:T(8,128)(2,1)S(1)} %bitcast.59), channel_id=1, source_target_pairs={{2,4},{4,2},{3,5},{5,3},{10,12},{12,10},{11,13},{13,11},{18,20},{2... | collective-permute-start | bytes 786440 | tf_op jit(solution)/shard_map/ppermute | solution.py:451
  35.9 4.3 %collective-permute-start.6 = (bf16[512,256]{1,0:T(8,128)(2,1)S(1)}, bf16[512,256]{1,0:T(8,128)(2,1)S(1)}, u32[]{:S(2)}, u32[]{:S(2)}) collective-permute-start(bf16[512,256]{1,0:T(8,128)(2,1)S(1)} %bitcast.58), channel_id=1, source_target_pairs={{2,4},{4,2},{3,5},{5,3},{10,12},{12,10},{11,13},{13,11},{18,20},{2... | collective-permute-start | bytes 786440 | tf_op jit(solution)/shard_map/ppermute | solution.py:451
  38.9 23.7 %collective-permute-start.8 = (bf16[512,256]{1,0:T(8,128)(2,1)S(1)}, bf16[512,256]{1,0:T(8,128)(2,1)S(1)}, u32[]{:S(2)}, u32[]{:S(2)}) collective-permute-start(bf16[512,256]{1,0:T(8,128)(2,1)S(1)} %collective-permute-done.5.refs_2_), channel_id=1, source_target_pairs={{2,0},{4,6},{3,1},{5,7},{10,8},{12,14},{11,9},{13,15},{18,16},{20,... | collective-permute-start | bytes 786440 | tf_op jit(solution)/shard_map/ppermute | solution.py:458
  40.2 25.2 %collective-permute-start.7 = (bf16[512,256]{1,0:T(8,128)(2,1)S(1)}, bf16[512,256]{1,0:T(8,128)(2,1)S(1)}, u32[]{:S(2)}, u32[]{:S(2)}) collective-permute-start(bf16[512,256]{1,0:T(8,128)(2,1)S(1)} %collective-permute-done.6.refs_0_), channel_id=1, source_target_pairs={{2,0},{4,6},{3,1},{5,7},{10,8},{12,14},{11,9},{13,15},{18,16},{20,... | collective-permute-start | bytes 786440 | tf_op jit(solution)/shard_map/ppermute | solution.py:458
